TPU v7x, 32 devices: a whole 2x2x4 slice. The times are simulated.
32 devices in a mesh: seq: 8 (over z, y), tp: 4 (over x, core).
Axes of the slice: x: 2, y: 2, z: 4, core: 2. Of those that a mesh axis runs over, the one named last changes fastest.
Arguments:
- tokens: bfloat16 [1024, 2048], P('seq'), may hold values from -6 to 6
- norm_gain: float32 [2048], replicated, may hold values from 0.5 to 1.5
- w_x: bfloat16 [2048, 2048], P(None, 'tp'), may hold values from -0.125 to 0.125
- w_z: bfloat16 [2048, 2048], P(None, 'tp'), may hold values from -0.125 to 0.125
- conv_w: float32 [4, 2048], P(None, 'tp'), may hold values from -3 to 3
- conv_b: float32 [2048], P('tp'), may hold values from -0.5 to 0.5
- w_xproj: bfloat16 [2048, 160], P('tp'), may hold values from -0.125 to 0.125
- w_dt: bfloat16 [128, 2048], P(None, 'tp'), may hold values from -0.5 to 0.5
- dt_bias: float32 [2048], P('tp'), may hold values from -4.6 to -3.4
- a_log: float32 [16, 2048], P(None, 'tp'), may hold values from -3.9 to -0.7
- d_skip: float32 [2048], P('tp'), may hold values from 0.5 to 1.5
- w_out: bfloat16 [2048, 2048], P('tp'), may hold values from -0.125 to 0.125
- mlp_gain: float32 [2048], replicated, may hold values from 0.5 to 1.5
- w_gate: bfloat16 [2048, 4096], P(None, 'tp'), may hold values from -0.125 to 0.125
- w_up: bfloat16 [2048, 4096], P(None, 'tp'), may hold values from -0.125 to 0.125
- w_down: bfloat16 [4096, 2048], P('tp'), may hold values from -0.09375 to 0.09375
- prompt_lengths: int32 [4], replicated, may hold values from 1 to 512, as said below
- request_prompt: int32 [32], P('seq'), may hold values from 0 to 3, as said below
Outputs:
- mixed_out: bfloat16 [1024, 2048], P(('seq', 'tp'))
- req_states: float32 [32, 16, 2048], P('seq', None, 'tp')
- req_edges: bfloat16 [32, 3, 2048], P('seq', None, 'tp')
Inputs may be any that keep to these rules, and one draw needn't show every extreme that they name: `prompt_lengths`: the prompts are packed in order from slot 0 and sum to 960 tokens; the remaining slots are padding; the last prompt is exactly 512 long. `request_prompt`: every prompt is continued by at least one request.
All inputs are finite; a program needn't handle non-finite values.
Results may differ from a plain program's by a relative error of at most 0.025.
Values may be sent and summed in bfloat16 or wider, within the bound.
A program may use at most 128 MiB of HBM per device.

v0:
```python
import jax
import jax.numpy as jnp
from jax import lax
from jax.experimental import pallas as pl
from jax.experimental.pallas import tpu as pltpu
from jax.sharding import PartitionSpec as P

EPSILON = 1e-05
F32 = jnp.float32
BF16 = jnp.bfloat16
FAR = 1e30
GROUP = 8


def rms_norm(values, gain):
    scale = lax.rsqrt(jnp.mean(values * values, axis=-1, keepdims=True) + EPSILON)
    return values * scale * gain


def silu(v):
    return v * jax.nn.sigmoid(v)


def dot(a, b):
    return jnp.dot(a, b, preferred_element_type=F32)


def remote(src, dst, send_sem, recv_sem, device):
    return pltpu.make_async_remote_copy(
        src_ref=src,
        dst_ref=dst,
        send_sem=send_sem,
        recv_sem=recv_sem,
        device_id=device,
        device_id_type=pl.DeviceIdType.MESH,
    )


NAMES = (
    "tokens", "norm_gain", "w_x", "w_z", "conv_w", "conv_b", "w_xproj", "w_dt", "dt_bias",
    "a_log", "d_skip", "w_out", "mlp_gain", "w_gate", "w_up", "w_down",
)
EARLY = NAMES[:3]
LATE = ("w_out", "w_gate", "w_up", "w_down")
NEXT = tuple(k for k in NAMES if k not in EARLY + LATE)


def make_local(S, T):
    X = T // 2

    def local(*args):
        arrays = dict(zip(NAMES, args[:16]))
        prompt_lengths, request_prompt = args[16:]
        for k in ("norm_gain", "conv_b", "dt_bias", "d_skip", "mlp_gain"):
            arrays[k] = arrays[k][None, :]
        B, D = arrays["tokens"].shape
        E = arrays["w_x"].shape[1]
        K = arrays["conv_w"].shape[0]
        R = arrays["w_dt"].shape[0]
        N = arrays["a_log"].shape[0]
        M = arrays["w_xproj"].shape[1]
        FF = arrays["w_gate"].shape[1]
        NP = prompt_lengths.shape[0]
        NR = request_prompt.shape[0]
        rc = B // T
        J = K - 1
        EP = -(-NP * J // 16) * 16
        FR = NP * N + EP
        groups = B // GROUP

        scratch = {k: pltpu.VMEM(arrays[k].shape, arrays[k].dtype) for k in NAMES}
        scratch.update(
            load_sem=pltpu.SemaphoreType.DMA((16,)),
            edge_s=pltpu.VMEM((16, E), BF16),
            edge_r=pltpu.VMEM((16, E), BF16),
            edge_sem=pltpu.SemaphoreType.DMA((2,)),
            ext=pltpu.VMEM((8 + B, E), F32),
            z=pltpu.VMEM((B, E), F32),
            pj=pltpu.VMEM((T, B, M), BF16),
            pj_send=pltpu.SemaphoreType.DMA((T,)),
            pj_recv=pltpu.SemaphoreType.DMA((T,)),
            mp=pltpu.VMEM((B, 256), F32),
            m3=pltpu.VMEM((groups, 2 * N, GROUP), F32),
            stepd=pltpu.VMEM((B, E), F32),
            drv=pltpu.VMEM((B, E), F32),
            dec=pltpu.VMEM((B, N, E), F32),
            sts=pltpu.VMEM((B, N, E), F32),
            y=pltpu.VMEM((B, E), F32),
            ssum=pltpu.VMEM((S, 1, E), F32),
            sbuf=pltpu.VMEM((S, N, E), BF16),
            a_send=pltpu.SemaphoreType.DMA((S,)),
            a_recv=pltpu.SemaphoreType.DMA((S,)),
            b_send=pltpu.SemaphoreType.DMA((S,)),
            b_recv=pltpu.SemaphoreType.DMA((S,)),
            fin=pltpu.VMEM((S, FR, E), BF16),
            f_send=pltpu.SemaphoreType.DMA((S,)),
            f_recv=pltpu.SemaphoreType.DMA((S,)),
            stat=pltpu.VMEM((NP, N, E), F32),
            edg=pltpu.VMEM((NP, 8, E), F32),
            part=pltpu.VMEM((2, X, rc, D), BF16),
            recv1=pltpu.VMEM((X, rc, D), BF16),
            psb=pltpu.VMEM((X, rc, D), BF16),
            recv2=pltpu.VMEM((X, X, rc, D), BF16),
            res=pltpu.VMEM((X, rc, D), F32),
            n2=pltpu.VMEM((2, X, rc, D), BF16),
            hid=pltpu.VMEM((B, FF), BF16),
            partb=pltpu.VMEM((2, X, rc, D), BF16),
            recv3=pltpu.VMEM((X, rc, D), BF16),
            psb2=pltpu.VMEM((X, rc, D), BF16),
            recv4=pltpu.VMEM((X, rc, D), BF16),
            c_send=pltpu.SemaphoreType.DMA((3,)),
            c_recv=pltpu.SemaphoreType.DMA((3,)),
            x_send=pltpu.SemaphoreType.DMA((2, X)),
            x_recv=pltpu.SemaphoreType.DMA((2, X)),
        )
        keys = list(scratch)

        def kernel(*refs):
            hbm = dict(zip(NAMES, refs[:16]))
            lens, reqs, out, out_states, out_edges = refs[16:21]
            s = dict(zip(keys, refs[21:]))
            seq = lax.axis_index("seq")
            tp = lax.axis_index("tp")
            x = lax.div(tp, 2)
            c = lax.rem(tp, 2)
            sib = {"tp": x * 2 + 1 - c}

            loads = {
                k: pltpu.make_async_copy(hbm[k], s[k], s["load_sem"].at[i])
                for i, k in enumerate(NAMES)
            }
            for k in EARLY:
                loads[k].start()

            barrier = pltpu.get_barrier_semaphore()
            for i in range(1, T):
                pl.semaphore_signal(
                    barrier, 1, device_id={"tp": lax.rem(tp + i, T)},
                    device_id_type=pl.DeviceIdType.MESH,
                )

            @pl.loop(1, S)
            def _(i):
                pl.semaphore_signal(
                    barrier, 1, device_id={"seq": lax.rem(seq + i, S)},
                    device_id_type=pl.DeviceIdType.MESH,
                )

            for k in NEXT:
                loads[k].start()

            ends, starts = [], []
            total = jnp.int32(0)
            for p in range(NP):
                starts.append(total)
                total = total + lens[p]
                ends.append(total)
            first = seq * B
            places = first + lax.broadcasted_iota(jnp.int32, (B, 1), 0)
            start_of = jnp.zeros((B, 1), jnp.int32)
            begins = jnp.zeros((B, 1), jnp.int32)
            for p in range(NP):
                here = (places >= starts[p]) & (places < ends[p])
                start_of = jnp.where(here, starts[p], start_of)
                begins = jnp.where(places == starts[p], 1, begins)
            offset = places - start_of

            loads["tokens"].wait()
            loads["norm_gain"].wait()
            normed = rms_norm(s["tokens"][...].astype(F32), s["norm_gain"][...]).astype(BF16)
            loads["w_x"].wait()
            for k in LATE:
                loads[k].start()
            xb = dot(normed, s["w_x"][...]).astype(BF16)
            s["edge_s"][...] = xb[B - 16 :]
            xf = xb.astype(F32)
            s["ext"][8:, :] = xf
            pl.semaphore_wait(barrier, T - 1 + S - 1)
            edge = remote(
                s["edge_s"], s["edge_r"], s["edge_sem"].at[0], s["edge_sem"].at[1],
                {"seq": lax.rem(seq + 1, S)},
            )

            @pl.when(seq < S - 1)
            def _():
                edge.start()

            for k in NEXT:
                loads[k].wait()
            half = E // 2
            s["z"][:, :half] = dot(normed, s["w_z"][:, :half])

            @pl.when(seq > 0)
            def _():
                edge.wait_recv()
                s["ext"][0:8, :] = s["edge_r"][...].astype(F32)[8:]

            @pl.when(seq == 0)
            def _():
                s["ext"][0:8, :] = jnp.zeros((8, E), F32)

            acc = jnp.zeros((B, E), F32) + s["conv_b"][...]
            for lag in range(K):
                window = s["ext"][8 - lag : 8 - lag + B, :]
                mask = jnp.where(offset >= lag, 1.0, 0.0)
                acc = acc + s["conv_w"][J - lag : J - lag + 1, :] * window * mask
            conv_out = silu(acc).astype(BF16)

            s["pj"][0] = dot(conv_out, s["w_xproj"][...]).astype(BF16)
            pj = []
            for i in range(1, T):
                pj.append(
                    remote(
                        s["pj"].at[0], s["pj"].at[i], s["pj_send"].at[i], s["pj_recv"].at[i],
                        {"tp": lax.rem(tp + i, T)},
                    )
                )
                pj[-1].start()
            s["z"][:, half:] = dot(normed, s["w_z"][:, half:])
            rates = -jnp.exp(s["a_log"][...])
            conv = conv_out.astype(F32)
            s["mp"][...] = jnp.zeros((B, 256), F32)
            projected = s["pj"][0].astype(F32)
            for i in range(1, T):
                pj[i - 1].wait_recv()
                projected = projected + s["pj"][i].astype(F32)
            s["mp"][:, :M] = projected
            maps = jnp.transpose(s["mp"][:, R : R + 128])
            for g in range(groups):
                s["m3"][g] = maps[: 2 * N, g * GROUP : (g + 1) * GROUP]
            low = s["mp"][:, :R].astype(BF16)
            pre = dot(low, s["w_dt"][...]) + s["dt_bias"][...]
            step = jnp.maximum(pre, 0.0) + jnp.log1p(jnp.exp(-jnp.abs(pre)))
            s["drv"][...] = step * conv
            stepd = jnp.where(begins > 0, FAR, step)
            s["stepd"][...] = stepd
            s["ssum"][seq] = jnp.sum(stepd, axis=0, keepdims=True)

            def send_a(d):
                return remote(
                    s["ssum"].at[seq], s["ssum"].at[seq], s["a_send"].at[d],
                    s["a_recv"].at[seq], {"seq": d},
                )

            def send_b(d):
                return remote(
                    s["sbuf"].at[seq], s["sbuf"].at[seq], s["b_send"].at[d],
                    s["b_recv"].at[seq], {"seq": d},
                )

            @pl.loop(seq + 1, S)
            def _(d):
                send_a(d).start()

            def one(g, st):
                base = pl.multiple_of(g * GROUP, GROUP)
                sg = s["stepd"][pl.ds(base, GROUP), :]
                dg = s["drv"][pl.ds(base, GROUP), :]
                mg = s["m3"][g]
                for i in range(GROUP):
                    decay = jnp.exp(sg[i : i + 1, :] * rates)
                    s["dec"][base + i] = decay
                    st = decay * st + dg[i : i + 1, :] * mg[:N, i : i + 1]
                return st

            last = lax.fori_loop(0, groups, one, jnp.zeros((N, E), F32))
            s["sbuf"][seq] = last.astype(BF16)

            @pl.loop(seq + 1, S)
            def _(d):
                send_b(d).start()

            s["z"][...] = silu(s["z"][...].astype(BF16).astype(F32))

            def join(e, st):
                remote(
                    s["ssum"].at[e], s["ssum"].at[e], s["a_send"].at[e], s["a_recv"].at[e],
                    {"seq": e},
                ).wait_recv()
                remote(
                    s["sbuf"].at[e], s["sbuf"].at[e], s["b_send"].at[e], s["b_recv"].at[e],
                    {"seq": e},
                ).wait_recv()
                return jnp.exp(s["ssum"][e] * rates) * st + s["sbuf"][e].astype(F32)

            state_in = lax.fori_loop(0, seq, join, jnp.zeros((N, E), F32))

            def two(g, st):
                base = pl.multiple_of(g * GROUP, GROUP)
                dg = s["drv"][pl.ds(base, GROUP), :]
                mg = s["m3"][g]
                rows = []
                for i in range(GROUP):
                    st = s["dec"][base + i] * st + dg[i : i + 1, :] * mg[:N, i : i + 1]
                    s["sts"][base + i] = st
                    rows.append(jnp.sum(st * mg[N:, i : i + 1], axis=0, keepdims=True))
                s["y"][pl.ds(base, GROUP), :] = jnp.concatenate(rows, axis=0)
                return st

            lax.fori_loop(0, groups, two, state_in)
            gated = ((s["y"][...] + s["d_skip"][...] * conv) * s["z"][...]).astype(BF16)

            loads["w_out"].wait()
            cols = min(D, 512)

            def project_out(left, w, dest, permuted):
                @pl.loop(0, D // cols)
                def _(j):
                    at = pl.ds(pl.multiple_of(j * cols, cols), cols)
                    val = dot(left(), w[:, at]).astype(BF16)
                    for q in range(T):
                        rows = val[q * rc : (q + 1) * rc]
                        if permuted:
                            dest[q // X, q % X, :, at] = rows
                        else:
                            dest[q % 2, q // 2, :, at] = rows

            s["hid"][:, :E] = gated
            project_out(lambda: s["hid"][:, :E], s["w_out"], s["part"], False)
            first_sum = remote(
                s["part"].at[1 - c], s["recv1"], s["c_send"].at[0], s["c_recv"].at[0], sib
            )
            first_sum.start()

            for p in range(NP):
                row = jnp.clip(ends[p] - 1 - first, 0, B - 1)
                s["fin"][seq, p * N : (p + 1) * N, :] = s["sts"][row].astype(BF16)
            rows = []
            for p in range(NP):
                for j in range(J):
                    target = jnp.clip(ends[p] - J + j - first + 8, 0, B + 7)
                    got = s["ext"][pl.ds(target, 1), :]
                    rows.append(jnp.where(ends[p] - J + j >= starts[p], got, 0.0))
            rows += [jnp.zeros((1, E), F32)] * (EP - NP * J)
            s["fin"][seq, NP * N :, :] = jnp.concatenate(rows, axis=0).astype(BF16)

            def send_f(i):
                return remote(
                    s["fin"].at[seq], s["fin"].at[seq], s["f_send"].at[i], s["f_recv"].at[seq],
                    {"seq": lax.rem(seq + i, S)},
                )

            @pl.loop(1, S)
            def _(i):
                send_f(i).start()

            first_sum.wait_recv()
            s["psb"][...] = (s["part"][c].astype(F32) + s["recv1"][...].astype(F32)).astype(BF16)
            over_x = []
            for i in range(1, X):
                over_x.append(
                    remote(
                        s["psb"], s["recv2"].at[i], s["x_send"].at[0, i], s["x_recv"].at[0, i],
                        {"tp": lax.rem(x + i, X) * 2 + c},
                    )
                )
                over_x[-1].start()
            for r in over_x:
                r.wait_recv()
            for b in range(X):
                at = pl.ds(pl.multiple_of((2 * b + c) * rc, rc), rc)
                val = s["tokens"][at, :].astype(F32) + s["psb"][b].astype(F32)
                for i in range(1, X):
                    val = val + s["recv2"][i, b].astype(F32)
                s["res"][b] = val
                s["n2"][c, b] = rms_norm(val, s["mlp_gain"][...]).astype(BF16)
            swap = remote(
                s["n2"].at[c], s["n2"].at[c], s["c_send"].at[1], s["c_recv"].at[1], sib
            )
            swap.start()
            for k in ("w_gate", "w_up", "w_down"):
                loads[k].wait()
            swap.wait_recv()

            wide = min(FF, 256)

            @pl.loop(0, FF // wide)
            def _(j):
                at = pl.ds(pl.multiple_of(j * wide, wide), wide)
                left = s["n2"][...].reshape(B, D)
                gate = dot(left, s["w_gate"][:, at])
                up = dot(left, s["w_up"][:, at])
                s["hid"][:, at] = (silu(gate) * up).astype(BF16)

            project_out(lambda: s["hid"][...], s["w_down"], s["partb"], True)
            second_sum = remote(
                s["partb"].at[1 - c], s["recv3"], s["c_send"].at[2], s["c_recv"].at[2], sib
            )
            second_sum.start()
            second_sum.wait_recv()
            s["psb2"][...] = (s["partb"][c].astype(F32) + s["recv3"][...].astype(F32)).astype(BF16)
            back = []
            for i in range(1, X):
                there = lax.rem(x + i, X)
                back.append(
                    remote(
                        s["psb2"].at[there], s["recv4"].at[i], s["x_send"].at[1, i],
                        s["x_recv"].at[1, i], {"tp": there * 2 + c},
                    )
                )
                back[-1].start()

            @pl.loop(1, S)
            def _(i):
                e = lax.rem(seq + i, S)
                remote(
                    s["fin"].at[e], s["fin"].at[e], s["f_send"].at[i], s["f_recv"].at[e],
                    {"seq": e},
                ).wait_recv()

            for p in range(NP):
                owner = lax.div(ends[p] - 1, B)
                got = s["fin"][owner]
                s["stat"][p] = got[p * N : (p + 1) * N].astype(F32)
                s["edg"][p, 0:J, :] = got[NP * N :].astype(F32)[p * J : (p + 1) * J]
            for r in range(NR):
                out_states[r] = s["stat"][reqs[r]]
                out_edges[r] = s["edg"][reqs[r], 0:J, :]

            val = s["res"][x] + s["psb2"][x].astype(F32)
            for i in range(1, X):
                back[i - 1].wait_recv()
                val = val + s["recv4"][i].astype(F32)
            slot = first + tp * rc + lax.broadcasted_iota(jnp.int32, (rc, 1), 0)
            out[...] = (val * jnp.where(slot < total, 1.0, 0.0)).astype(BF16)

            @pl.when(seq < S - 1)
            def _():
                edge.wait_send()

            for r in pj + over_x + back + [first_sum, swap, second_sum]:
                r.wait_send()

            @pl.loop(seq + 1, S)
            def _(d):
                send_a(d).wait_send()
                send_b(d).wait_send()

            @pl.loop(1, S)
            def _(i):
                send_f(i).wait_send()

        anyspec = pl.BlockSpec(memory_space=pl.ANY)
        smem = pl.BlockSpec(memory_space=pltpu.SMEM)
        vmem = pl.BlockSpec(memory_space=pltpu.VMEM)
        mixed_out, req_states, req_edges = pl.pallas_call(
            kernel,
            out_shape=(
                jax.ShapeDtypeStruct((rc, D), BF16),
                jax.ShapeDtypeStruct((NR, N, E), F32),
                jax.ShapeDtypeStruct((NR, J, E), F32),
            ),
            in_specs=[anyspec] * 16 + [smem] * 2,
            out_specs=(vmem,) * 3,
            scratch_shapes=list(scratch.values()),
            compiler_params=pltpu.CompilerParams(
                collective_id=0, has_side_effects=True, vmem_limit_bytes=58 * 2**20
            ),
        )(*[arrays[k] for k in NAMES], prompt_lengths, request_prompt)
        return mixed_out, req_states, req_edges.astype(BF16)

    return local


def solution(mesh):
    placed = (
        P("seq", None),
        P(),
        P(None, "tp"),
        P(None, "tp"),
        P(None, "tp"),
        P("tp"),
        P("tp", None),
        P(None, "tp"),
        P("tp"),
        P(None, "tp"),
        P("tp"),
        P("tp", None),
        P(),
        P(None, "tp"),
        P(None, "tp"),
        P("tp", None),
        P(),
        P("seq"),
    )
    return jax.shard_map(
        make_local(mesh.shape["seq"], mesh.shape["tp"]),
        mesh=mesh,
        in_specs=placed,
        out_specs=(P(("seq", "tp"), None), P("seq", None, "tp"), P("seq", None, "tp")),
        check_vma=False,
    )
```

profile of v0, /device:TPU:24, one launch (start us, length us, event | category | flops | bytes accessed | tf_op | source)
XLA Modules:
  0.0 49.2 jit_solution(5184812193809781575)
XLA Ops:
  0.6 1.7 %copy.21.refs_6_ = bf16[512,160]{1,0:T(8,128)(2,1)} copy(bf16[512,160]{0,1:T(8,128)(2,1)} %param.24) | data formatting | bytes 327680 | tf_op args[6]
  2.4 42.3 %shard_map.193 = (bf16[32,2048]{1,0:T(8,128)(2,1)}, f32[4,16,512]{2,1,0:T(8,128)}, f32[4,3,512]{2,1,0:T(4,128)}) custom-call(bf16[128,2048]{1,0:T(8,128)(2,1)} %refs_0_.1, f32[1,2048]{1,0:T(1,128)} %bitcast.5, bf16[2048,512]{1,0:T(8,128)(2,1)} %refs_2_.1, bf16[2048,512]{1,0:T(8,128)(2,1)} %refs_3_.1, f32[4,512]{1,0:T(4,128)} %refs_4_.1, f32[1,512]{1,0:T(1,128)} %bitcast.7, ...), custom_call_target="tpu_custom_call" | custom-call | tf_op jit(solution)/shard_map/pallas_call | solution.py:446
  44.7 0.8 %convert_element_type.3 = bf16[4,3,512]{2,1,0:T(4,128)(2,1)S(1)} convert(f32[4,3,512]{2,1,0:T(4,128)} %get-tuple-element.8) | non-fusion elementwise | flops 6144 | bytes 36864 | tf_op jit(solution)/shard_map/convert_element_type | solution.py:460
  45.5 0.6 %copy.22 = bf16[4,3,512]{2,0,1:T(4,128)(2,1)} copy(bf16[4,3,512]{2,1,0:T(4,128)(2,1)S(1)} %convert_element_type.3) | data formatting | bytes 24576
  46.1 1.6 %copy.25 = bf16[32,2048]{1,0:T(8,128)(2,1)} copy(bf16[32,2048]{1,0:T(8,128)(2,1)} %get-tuple-element.15) | data formatting | bytes 262144
  47.7 1.6 %copy.26 = f32[4,16,512]{2,1,0:T(8,128)} copy(f32[4,16,512]{2,1,0:T(8,128)} %get-tuple-element.16) | data formatting | bytes 262144
where the time goes:
time: 49.5 us; the launch traced here: 49.2 us
  Pallas kernels  42.3 us (85%)
  local copies, waits for them, and re-layouts  5.49 us (11%)
  other arithmetic  0.77 us (2%)
  between operations  0.64 us (1%)
    pallas_call x1, Pallas kernels, local(): pl.pallas_call(kernel, out_shape=(jax.ShapeDtypeStruct((rc, D), BF16), ja...  42.3 us
    unnamed x4, local copies, waits for them, and re-layouts  5.49 us

commit v1 on v0

--- a/solution.py
+++ b/solution.py
@@ -59,6 +59,7 @@
         R = arrays["w_dt"].shape[0]
         N = arrays["a_log"].shape[0]
         M = arrays["w_xproj"].shape[1]
+        arrays["w_xproj"] = arrays["w_xproj"].T
         FF = arrays["w_gate"].shape[1]
         NP = prompt_lengths.shape[0]
         NR = request_prompt.shape[0]
@@ -67,6 +68,8 @@
         EP = -(-NP * J // 16) * 16
         FR = NP * N + EP
         groups = B // GROUP
+        cw = min(D, 512)
+        CH = D // cw
 
         scratch = {k: pltpu.VMEM(arrays[k].shape, arrays[k].dtype) for k in NAMES}
         scratch.update(
@@ -97,21 +100,22 @@
             f_recv=pltpu.SemaphoreType.DMA((S,)),
             stat=pltpu.VMEM((NP, N, E), F32),
             edg=pltpu.VMEM((NP, 8, E), F32),
-            part=pltpu.VMEM((2, X, rc, D), BF16),
-            recv1=pltpu.VMEM((X, rc, D), BF16),
-            psb=pltpu.VMEM((X, rc, D), BF16),
-            recv2=pltpu.VMEM((X, X, rc, D), BF16),
+            part=pltpu.VMEM((CH, 2, X, rc, cw), BF16),
+            recv1=pltpu.VMEM((CH, X, rc, cw), BF16),
+            psb=pltpu.VMEM((CH, X, rc, cw), BF16),
+            recv2=pltpu.VMEM((X, CH, X, rc, cw), BF16),
             res=pltpu.VMEM((X, rc, D), F32),
             n2=pltpu.VMEM((2, X, rc, D), BF16),
             hid=pltpu.VMEM((B, FF), BF16),
-            partb=pltpu.VMEM((2, X, rc, D), BF16),
-            recv3=pltpu.VMEM((X, rc, D), BF16),
-            psb2=pltpu.VMEM((X, rc, D), BF16),
-            recv4=pltpu.VMEM((X, rc, D), BF16),
-            c_send=pltpu.SemaphoreType.DMA((3,)),
-            c_recv=pltpu.SemaphoreType.DMA((3,)),
-            x_send=pltpu.SemaphoreType.DMA((2, X)),
-            x_recv=pltpu.SemaphoreType.DMA((2, X)),
+            partb=pltpu.VMEM((CH, 2, X, rc, cw), BF16),
+            recv3=pltpu.VMEM((CH, X, rc, cw), BF16),
+            psb2=pltpu.VMEM((CH, X, rc, cw), BF16),
+            recv4=pltpu.VMEM((X, CH, rc, cw), BF16),
+            swap_sem=pltpu.SemaphoreType.DMA((2,)),
+            c_send=pltpu.SemaphoreType.DMA((2, CH)),
+            c_recv=pltpu.SemaphoreType.DMA((2, CH)),
+            x_send=pltpu.SemaphoreType.DMA((2, CH, X)),
+            x_recv=pltpu.SemaphoreType.DMA((2, CH, X)),
         )
         keys = list(scratch)
 
@@ -206,7 +210,10 @@
                 acc = acc + s["conv_w"][J - lag : J - lag + 1, :] * window * mask
             conv_out = silu(acc).astype(BF16)
 
-            s["pj"][0] = dot(conv_out, s["w_xproj"][...]).astype(BF16)
+            s["pj"][0] = lax.dot_general(
+                conv_out, s["w_xproj"][...], (((1,), (1,)), ((), ())),
+                preferred_element_type=F32,
+            ).astype(BF16)
             pj = []
             for i in range(1, T):
                 pj.append(
@@ -301,26 +308,47 @@
             gated = ((s["y"][...] + s["d_skip"][...] * conv) * s["z"][...]).astype(BF16)
 
             loads["w_out"].wait()
-            cols = min(D, 512)
-
-            def project_out(left, w, dest, permuted):
-                @pl.loop(0, D // cols)
-                def _(j):
-                    at = pl.ds(pl.multiple_of(j * cols, cols), cols)
-                    val = dot(left(), w[:, at]).astype(BF16)
-                    for q in range(T):
-                        rows = val[q * rc : (q + 1) * rc]
-                        if permuted:
-                            dest[q // X, q % X, :, at] = rows
-                        else:
-                            dest[q % 2, q // 2, :, at] = rows
-
             s["hid"][:, :E] = gated
-            project_out(lambda: s["hid"][:, :E], s["w_out"], s["part"], False)
-            first_sum = remote(
-                s["part"].at[1 - c], s["recv1"], s["c_send"].at[0], s["c_recv"].at[0], sib
-            )
-            first_sum.start()
+            sums = ([], [])
+            over_x = ([], [])
+
+            def chunk(j):
+                return slice(j * cw, (j + 1) * cw)
+
+            def in_chip(k, j, left, w, dest, land, place_of):
+                val = dot(left, w[:, chunk(j)]).astype(BF16)
+                for q in range(T):
+                    cc, xx = place_of(q)
+                    dest[j, cc, xx] = val[q * rc : (q + 1) * rc]
+                r = remote(
+                    dest.at[j, 1 - c], land.at[j], s["c_send"].at[k, j], s["c_recv"].at[k, j], sib
+                )
+                r.start()
+                sums[k].append(r)
+
+            def pair_sum(k, j, part, land, dest):
+                sums[k][j].wait_recv()
+                dest[j] = (part[j, c].astype(F32) + land[j].astype(F32)).astype(BF16)
+                for i in range(1, X):
+                    there = lax.rem(x + i, X)
+                    r = remote(
+                        dest.at[j] if k == 0 else dest.at[j, there],
+                        s["recv2" if k == 0 else "recv4"].at[i, j],
+                        s["x_send"].at[k, j, i],
+                        s["x_recv"].at[k, j, i],
+                        {"tp": there * 2 + c},
+                    )
+                    r.start()
+                    over_x[k].append(r)
+
+            for j in range(CH + 1):
+                if j < CH:
+                    in_chip(
+                        0, j, s["hid"][:, :E], s["w_out"], s["part"], s["recv1"],
+                        lambda q: (q % 2, q // 2),
+                    )
+                if j > 0:
+                    pair_sum(0, j - 1, s["part"], s["recv1"], s["psb"])
 
             for p in range(NP):
                 row = jnp.clip(ends[p] - 1 - first, 0, B - 1)
@@ -344,28 +372,19 @@
             def _(i):
                 send_f(i).start()
 
-            first_sum.wait_recv()
-            s["psb"][...] = (s["part"][c].astype(F32) + s["recv1"][...].astype(F32)).astype(BF16)
-            over_x = []
-            for i in range(1, X):
-                over_x.append(
-                    remote(
-                        s["psb"], s["recv2"].at[i], s["x_send"].at[0, i], s["x_recv"].at[0, i],
-                        {"tp": lax.rem(x + i, X) * 2 + c},
-                    )
-                )
-                over_x[-1].start()
-            for r in over_x:
-                r.wait_recv()
+            for j in range(CH):
+                for i in range(1, X):
+                    over_x[0][j * (X - 1) + i - 1].wait_recv()
+                for b in range(X):
+                    at = pl.ds(pl.multiple_of((2 * b + c) * rc, rc), rc)
+                    val = s["tokens"][at, chunk(j)].astype(F32) + s["psb"][j, b].astype(F32)
+                    for i in range(1, X):
+                        val = val + s["recv2"][i, j, b].astype(F32)
+                    s["res"][b, :, chunk(j)] = val
             for b in range(X):
-                at = pl.ds(pl.multiple_of((2 * b + c) * rc, rc), rc)
-                val = s["tokens"][at, :].astype(F32) + s["psb"][b].astype(F32)
-                for i in range(1, X):
-                    val = val + s["recv2"][i, b].astype(F32)
-                s["res"][b] = val
-                s["n2"][c, b] = rms_norm(val, s["mlp_gain"][...]).astype(BF16)
+                s["n2"][c, b] = rms_norm(s["res"][b], s["mlp_gain"][...]).astype(BF16)
             swap = remote(
-                s["n2"].at[c], s["n2"].at[c], s["c_send"].at[1], s["c_recv"].at[1], sib
+                s["n2"].at[c], s["n2"].at[c], s["swap_sem"].at[0], s["swap_sem"].at[1], sib
             )
             swap.start()
             for k in ("w_gate", "w_up", "w_down"):
@@ -382,23 +401,14 @@
                 up = dot(left, s["w_up"][:, at])
                 s["hid"][:, at] = (silu(gate) * up).astype(BF16)
 
-            project_out(lambda: s["hid"][...], s["w_down"], s["partb"], True)
-            second_sum = remote(
-                s["partb"].at[1 - c], s["recv3"], s["c_send"].at[2], s["c_recv"].at[2], sib
-            )
-            second_sum.start()
-            second_sum.wait_recv()
-            s["psb2"][...] = (s["partb"][c].astype(F32) + s["recv3"][...].astype(F32)).astype(BF16)
-            back = []
-            for i in range(1, X):
-                there = lax.rem(x + i, X)
-                back.append(
-                    remote(
-                        s["psb2"].at[there], s["recv4"].at[i], s["x_send"].at[1, i],
-                        s["x_recv"].at[1, i], {"tp": there * 2 + c},
+            for j in range(CH + 1):
+                if j < CH:
+                    in_chip(
+                        1, j, s["hid"][...], s["w_down"], s["partb"], s["recv3"],
+                        lambda q: (q // X, q % X),
                     )
-                )
-                back[-1].start()
+                if j > 0:
+                    pair_sum(1, j - 1, s["partb"], s["recv3"], s["psb2"])
 
             @pl.loop(1, S)
             def _(i):
@@ -415,20 +425,24 @@
                 s["edg"][p, 0:J, :] = got[NP * N :].astype(F32)[p * J : (p + 1) * J]
             for r in range(NR):
                 out_states[r] = s["stat"][reqs[r]]
-                out_edges[r] = s["edg"][reqs[r], 0:J, :]
-
-            val = s["res"][x] + s["psb2"][x].astype(F32)
-            for i in range(1, X):
-                back[i - 1].wait_recv()
-                val = val + s["recv4"][i].astype(F32)
+                picked = s["edg"][reqs[r]]
+                for j in range(J):
+                    out_edges[j, r : r + 1, :] = picked[j : j + 1]
+
             slot = first + tp * rc + lax.broadcasted_iota(jnp.int32, (rc, 1), 0)
-            out[...] = (val * jnp.where(slot < total, 1.0, 0.0)).astype(BF16)
+            live = jnp.where(slot < total, 1.0, 0.0)
+            for j in range(CH):
+                val = s["res"][x, :, chunk(j)] + s["psb2"][j, x].astype(F32)
+                for i in range(1, X):
+                    over_x[1][j * (X - 1) + i - 1].wait_recv()
+                    val = val + s["recv4"][i, j].astype(F32)
+                out[:, chunk(j)] = (val * live).astype(BF16)
 
             @pl.when(seq < S - 1)
             def _():
                 edge.wait_send()
 
-            for r in pj + over_x + back + [first_sum, swap, second_sum]:
+            for r in pj + over_x[0] + over_x[1] + sums[0] + sums[1] + [swap]:
                 r.wait_send()
 
             @pl.loop(seq + 1, S)
@@ -448,7 +462,7 @@
             out_shape=(
                 jax.ShapeDtypeStruct((rc, D), BF16),
                 jax.ShapeDtypeStruct((NR, N, E), F32),
-                jax.ShapeDtypeStruct((NR, J, E), F32),
+                jax.ShapeDtypeStruct((J, NR, E), F32),
             ),
             in_specs=[anyspec] * 16 + [smem] * 2,
             out_specs=(vmem,) * 3,
@@ -457,7 +471,7 @@
                 collective_id=0, has_side_effects=True, vmem_limit_bytes=58 * 2**20
             ),
         )(*[arrays[k] for k in NAMES], prompt_lengths, request_prompt)
-        return mixed_out, req_states, req_edges.astype(BF16)
+        return mixed_out, req_states, jnp.transpose(req_edges.astype(BF16), (1, 0, 2))
 
     return local
 

time: 49.5 us -> 46 us (0.929)
  local copies, waits for them, and re-layouts: 5.49 us -> 3.13 us
  Pallas kernels: 42.3 us -> 40.6 us
  other arithmetic: 0.77 us -> 1.34 us
    unnamed x4 -> x2, local copies, waits for them, and re-layouts: 5.49 us -> 3.13 us
    pallas_call x1, Pallas kernels: 42.3 us -> 40.6 us  [local(): pl.pallas_call(kernel, out_shape=(jax.ShapeDtypeStruct((rc, D), BF16), ja...]
    transpose x0 -> x1, other arithmetic: none -> 1.34 us  [local(): jnp.transpose(req_edges.astype(BF16), (1, 0, 2))]
    convert_element_type x1 -> x0, other arithmetic: 0.77 us -> none  [local(): return (mixed_out, req_states, req_edges.astype(BF16))]
where the time goes in v1:
time: 46 us; the launch traced here: 45.7 us
  Pallas kernels  40.6 us (88%)
  local copies, waits for them, and re-layouts  3.13 us (7%)
  other arithmetic  1.34 us (3%)
  between operations  0.65 us (1%)
    pallas_call x1, Pallas kernels, local(): pl.pallas_call(kernel, out_shape=(jax.ShapeDtypeStruct((rc, D), BF16), ja...  40.6 us
    unnamed x2, local copies, waits for them, and re-layouts  3.13 us
    transpose x1, other arithmetic, local(): jnp.transpose(req_edges.astype(BF16), (1, 0, 2))  1.34 us

profile of v1, /device:TPU:24, one launch (start us, length us, event | category | flops | bytes accessed | tf_op | source)
XLA Modules:
  0.0 45.7 jit_solution(5419728958601057745)
XLA Ops:
  0.6 40.6 %shard_map.193 = (bf16[32,2048]{1,0:T(8,128)(2,1)}, f32[4,16,512]{2,1,0:T(8,128)}, f32[3,4,512]{2,1,0:T(4,128)}) custom-call(bf16[128,2048]{1,0:T(8,128)(2,1)} %refs_0_.1, f32[1,2048]{1,0:T(1,128)} %bitcast.9, bf16[2048,512]{1,0:T(8,128)(2,1)} %refs_2_.1, bf16[2048,512]{1,0:T(8,128)(2,1)} %refs_3_.1, f32[4,512]{1,0:T(4,128)} %refs_4_.1, f32[1,512]{1,0:T(1,128)} %bitcast.11, ...), custom_call_target="tpu_custom_call" | custom-call | tf_op jit(solution)/shard_map/pallas_call | solution.py:460
  41.2 1.3 %convert_bitcast_fusion = bf16[4,3,512]{2,0,1:T(4,128)(2,1)} fusion(f32[3,4,512]{2,1,0:T(4,128)} %get-tuple-element.8), kind=kLoop, calls=%fused_computation | loop fusion | flops 6144 | bytes 36864 | tf_op jit(solution)/shard_map/transpose | solution.py:474
  42.6 1.6 %copy.23 = bf16[32,2048]{1,0:T(8,128)(2,1)} copy(bf16[32,2048]{1,0:T(8,128)(2,1)} %get-tuple-element.12) | data formatting | bytes 262144
  44.1 1.6 %copy.24 = f32[4,16,512]{2,1,0:T(8,128)} copy(f32[4,16,512]{2,1,0:T(8,128)} %get-tuple-element.13) | data formatting | bytes 262144

commit v2 on v1

--- a/solution.py
+++ b/solution.py
@@ -471,7 +471,30 @@
                 collective_id=0, has_side_effects=True, vmem_limit_bytes=58 * 2**20
             ),
         )(*[arrays[k] for k in NAMES], prompt_lengths, request_prompt)
-        return mixed_out, req_states, jnp.transpose(req_edges.astype(BF16), (1, 0, 2))
+
+        def hand_over(mixed_in, states_in, edges_in, mixed, states, edges, sem):
+            copies = [
+                pltpu.make_async_copy(mixed_in, mixed, sem.at[0]),
+                pltpu.make_async_copy(states_in, states, sem.at[1]),
+            ]
+            for copy in copies:
+                copy.start()
+            edges[...] = edges_in[...].astype(BF16)
+            for copy in copies:
+                copy.wait()
+
+        mixed_out, req_states, req_edges = pl.pallas_call(
+            hand_over,
+            out_shape=(
+                jax.ShapeDtypeStruct((rc, D), BF16),
+                jax.ShapeDtypeStruct((NR, N, E), F32),
+                jax.ShapeDtypeStruct((J, NR, E), BF16),
+            ),
+            in_specs=[anyspec, anyspec, vmem],
+            out_specs=(anyspec, anyspec, vmem),
+            scratch_shapes=[pltpu.SemaphoreType.DMA((2,))],
+        )(mixed_out, req_states, req_edges)
+        return mixed_out, req_states, jnp.transpose(req_edges, (1, 0, 2))
 
     return local
 

time: 46 us -> 51.9 us (1.13)
  Pallas kernels: 40.6 us -> 50.9 us
  local copies, waits for them, and re-layouts: 3.13 us -> 0 us
  other arithmetic: 1.34 us -> 0 us
    pallas_call x0 -> x1, Pallas kernels: none -> 10.4 us  [local(): pl.pallas_call(hand_over, out_shape=(jax.ShapeDtypeStruct((rc, D), BF16),...]
    unnamed x2 -> x0, local copies, waits for them, and re-layouts: 3.13 us -> none
    transpose x1 -> x0, other arithmetic: 1.34 us -> none  [local(): jnp.transpose(req_edges.astype(BF16), (1, 0, 2))]
where the time goes in v2:
time: 51.9 us; the launch traced here: 51.6 us
  Pallas kernels  50.9 us (98%)
  between operations  0.65 us (1%)
    pallas_call x1, Pallas kernels, local(): pl.pallas_call(kernel, out_shape=(jax.ShapeDtypeStruct((rc, D), BF16), ja...  40.6 us
    pallas_call x1, Pallas kernels, local(): pl.pallas_call(hand_over, out_shape=(jax.ShapeDtypeStruct((rc, D), BF16),...  10.4 us

profile of v2, /device:TPU:24, one launch (start us, length us, event | category | flops | bytes accessed | tf_op | source)
XLA Modules:
  0.0 51.6 jit_solution(15380473876573138264)
XLA Ops:
  0.6 40.6 %shard_map.193 = (bf16[32,2048]{1,0:T(8,128)(2,1)}, f32[4,16,512]{2,1,0:T(8,128)}, f32[3,4,512]{2,1,0:T(4,128)}) custom-call(bf16[128,2048]{1,0:T(8,128)(2,1)} %refs_0_.1, f32[1,2048]{1,0:T(1,128)} %bitcast.8, bf16[2048,512]{1,0:T(8,128)(2,1)} %refs_2_.1, bf16[2048,512]{1,0:T(8,128)(2,1)} %refs_3_.1, f32[4,512]{1,0:T(4,128)} %refs_4_.1, f32[1,512]{1,0:T(1,128)} %bitcast.10, ...), custom_call_target="tpu_custom_call" | custom-call | tf_op jit(solution)/shard_map/pallas_call | solution.py:460
  41.2 10.4 %shard_map.194 = (bf16[32,2048]{1,0:T(8,128)(2,1)}, f32[4,16,512]{2,1,0:T(8,128)}, bf16[3,4,512]{2,1,0:T(4,128)(2,1)}) custom-call(bf16[32,2048]{1,0:T(8,128)(2,1)} %get-tuple-element.9.mixed_in, f32[4,16,512]{2,1,0:T(8,128)} %get-tuple-element.10.states_in, f32[3,4,512]{2,1,0:T(4,128)} %get-tuple-element.11.edges_in), custom_call_target="tpu_custom_call" | custom-call | tf_op jit(solution)/shard_map/pallas_call | solution.py:486
